TPU v7x, 128 devices: a whole 4x4x4 slice. The times are simulated.
128 devices in a mesh: row: 16 (over y, z_hi, core), col: 8 (over x, z_lo).
Axes of the slice: x: 4, y: 4, z: 4 (z_hi: 2, z_lo: 2; z = z_hi * 2 + z_lo), core: 2. Of those that a mesh axis runs over, the one named last changes fastest.
Arguments:
- pair_rep: bfloat16 [1024, 1024, 128], P('row', 'col'), may hold values from -6 to 6
- norm_gain: float32 [2, 128], replicated, may hold values from 0.1 to 1.9
- norm_bias: float32 [2, 128], replicated, may hold values from -3 to 3
- proj_weight: bfloat16 [2, 4, 128, 128], replicated, may hold values from -0.5 to 0.5
- gate_weight: bfloat16 [2, 128, 128], replicated, may hold values from -0.5 to 0.5
- out_gain: float32 [2, 128], replicated, may hold values from 0.1 to 1.9
- out_bias: float32 [2, 128], replicated, may hold values from -3 to 3
- out_weight: bfloat16 [2, 128, 128], replicated, may hold values from -0.5 to 0.5
Outputs:
- updated: bfloat16 [1024, 1024, 128], P('row', 'col')
All inputs are finite; a program needn't handle non-finite values.
Results may differ from a plain program's by a relative error of at most 0.008.
Values may be sent and summed in bfloat16 or wider, within the bound.
A program may use at most 64 MiB of HBM per device.

v0:
```python
import jax
import jax.numpy as jnp
from jax import lax
from jax.experimental import pallas as pl
from jax.experimental.pallas import tpu as pltpu
from jax.sharding import PartitionSpec as P

F32, BF16 = jnp.float32, jnp.bfloat16
ROWS, COLS, N_ROW, N_COL, CH = 64, 128, 16, 8, 128
DEV = N_ROW * N_COL
GROUP, HALF = 16, 32
MIB = 1 << 20
NT = (((1,), (1,)), ((), ()))
TN = (((0,), (0,)), ((), ()))
NN = (((1,), (0,)), ((), ()))
RIGHT, LEFT = 0, 1
PLACE = (
    {(k, half, g): 64 * k + 32 * half + 16 * g for k in range(2) for half in range(2) for g in range(2)},
    {
        (RIGHT, 0, 0): 0,
        (RIGHT, 0, 1): 16,
        (LEFT, 0, 0): 32,
        (RIGHT, 1, 0): 48,
        (RIGHT, 1, 1): 64,
        (LEFT, 1, 0): 80,
        (LEFT, 0, 1): 96,
        (LEFT, 1, 1): 112,
    },
)
SIDES = (
    (0, 0, 16), (0, 16, 16), (0, 32, 32), (0, 64, 32), (0, 96, 32),
    (1, 0, 16), (1, 16, 16), (1, 32, 16), (1, 48, 32), (1, 80, 16), (1, 96, 16), (1, 112, 16),
)
MIXED = ((0, 0, 16), (0, 16, 16), (0, 32, 16), (0, 48, 16), (1, 0, 32), (1, 32, 16), (1, 48, 16))
FLIGHTS = len(SIDES) + len(MIXED)


def sigmoid(v):
    return 0.5 * jnp.tanh(0.5 * v) + 0.5


def layer_norm(v, gain, bias):
    mean = jnp.mean(v, axis=-1, keepdims=True)
    centred = v - mean
    var = jnp.mean(centred * centred, axis=-1, keepdims=True)
    return centred * lax.rsqrt(var + 1e-5) * gain + bias


def dot(a, b, dims):
    return lax.dot_general(a, b, dims, preferred_element_type=F32)


def each_target(row, col, body):
    y, zh, k = row // 4, lax.rem(row // 2, 2), lax.rem(row, 2)
    x, zl = col // 2, lax.rem(col, 2)
    sign = 1 - 2 * k
    turns = [sign * a + 4 for a in range(4)]
    xs = [lax.rem(x + turn, 4) * 2 for turn in turns]
    ys = [lax.rem(y + turn, 4) * 4 for turn in turns]

    def sixteen(core, c, skip):
        core_at = lax.rem(k + core, 2)
        z = [lax.rem(zh * 2 + zl + sign * c + 4 + turn, 4) for turn in turns]
        z_rows = [(at // 2) * 2 + core_at for at in z]
        z_cols = [lax.rem(at, 2) for at in z]
        for b in range(4):
            for a in range(4):
                if not (skip and a == 0 and b == 0):
                    ab = (a + b) % 4
                    body(ys[ab] + z_rows[ab], xs[a] + z_cols[ab])

    def step(p, carry):
        sixteen(p // 4, lax.rem(p, 4), False)
        return carry

    sixteen(0, 0, True)
    lax.fori_loop(1, 8, step, 0)


def back_rows(mixed, cur, gate, new, gain_t, bias_t, weight, tl, ts):
    m = mixed.astype(F32)
    mean = jnp.mean(m, axis=0)
    centred = m - mean[None]
    var = jnp.mean(centred * centred, axis=0)
    ts[...] = lax.rsqrt(var + 1e-5)
    tl[...] = centred.reshape(CH * GROUP, COLS)
    for i in range(GROUP):
        c = tl[pl.ds(i, CH, stride=GROUP), :]
        nm = (c * ts[pl.ds(i, 1), :] * gain_t[...] + bias_t[...]).astype(BF16)
        change = dot(nm, weight[...], TN)
        new[i] = (cur[i].astype(F32) + gate[i] * change).astype(BF16)


def kernel(
    pair_h, ng_h, nb_h, pw_h, gw_h, og_h, ob_h, ow_h, out_h, last_mixed, last_gate, last_cur,
    cur, normed, gate, sides, all_sides, lt, acc, m_all, m_in,
    ng, nb, pw, gw, og, ob, ow, wt, gain_t, bias_t, tl, tr, ts,
    load_sem, param_sem, send_sem, recv_sem, out_sem, ahead_sem,
):
    row, col = lax.axis_index("row"), lax.axis_index("col")
    me = row * N_COL + col

    def load(g):
        rows = pl.ds(g * GROUP, GROUP)
        return pltpu.make_async_copy(pair_h.at[rows], cur.at[0, rows], load_sem.at[g])

    first = pl.ds(2, 2)
    params = [
        pltpu.make_async_copy(src, dst, param_sem.at[k])
        for k, (src, dst) in enumerate(
            (
                (pw_h.at[0, first], pw.at[0, first]),
                (ng_h, ng),
                (nb_h, nb),
                (pw_h.at[0, pl.ds(0, 2)], pw.at[0, pl.ds(0, 2)]),
                (pw_h.at[1], pw.at[1]),
                (gw_h, gw),
                (og_h, og),
                (ob_h, ob),
                (ow_h, ow),
            )
        )
    ]
    load(0).start()
    for copy in params[:3]:
        copy.start()
    for g in range(1, ROWS // GROUP):
        load(g).start()
    for copy in params[3:]:
        copy.start()

    barrier = pltpu.get_barrier_semaphore()

    def greet(r, c):
        pl.semaphore_signal(
            barrier, inc=1, device_id=(r, c), device_id_type=pl.DeviceIdType.MESH
        )

    each_target(row, col, greet)
    for copy in params[:3]:
        copy.wait()
    for k in range(2, 4):
        wt[0, k * CH : (k + 1) * CH] = pw[0, k].T

    def norm_rows(u, base):
        x = cur[u, pl.ds(base, 2)].reshape(2 * COLS, CH).astype(F32)
        n = layer_norm(x, ng[u : u + 1], nb[u : u + 1]).astype(BF16)
        normed[pl.ds(base, 2)] = n.reshape(2, COLS, CH)
        return n

    def project(u, k, n):
        first = 256 * (1 - k)
        p = dot(wt[u, first : first + 256], n, NT)
        return sigmoid(p[0:128]) * p[128:256]

    def keep(u, k, half, g, wide):
        first = PLACE[u][k, half, 0] + g * GROUP
        if (u, k) == (1, LEFT):
            first = PLACE[u][k, half, g]
        rows = pl.ds(pl.multiple_of(first, GROUP), GROUP)
        sides[u, :, rows, :] = wide[...].reshape(CH, GROUP, COLS).astype(BF16)

    def front_group(u, k, half, g, fresh=True):
        base = half * HALF + g * GROUP
        for i in range(0, GROUP, 2):
            if fresh:
                n = norm_rows(u, base + i)
            else:
                n = normed[pl.ds(base + i, 2)].reshape(2 * COLS, CH)
            side = project(u, k, n)
            for r in range(2):
                (tr, tl)[k][pl.ds(i + r, CH, stride=GROUP), :] = side[:, r * COLS : (r + 1) * COLS]
        keep(u, k, half, g, (tr, tl)[k])

    def left_by_parts(half):
        def eight(p):
            for q in range(8):
                rows = [half * HALF + p * 8 + q + r * GROUP for r in range(2)]
                order = [(r, c) for part in range(2) for r in rows for c in (part, part + 2)]
                n = jnp.concatenate([normed[r, c * 32 : (c + 1) * 32] for r, c in order], axis=0)
                side = project(1, LEFT, n)
                for part, wide in enumerate((tl, tr)):
                    wide[pl.ds(p * 8 + q, CH, stride=GROUP), :] = side[
                        :, part * COLS : (part + 1) * COLS
                    ]

        loop(2, eight)
        keep(1, LEFT, half, 0, tl)
        keep(1, LEFT, half, 1, tr)

    def gate_rows(u, step):
        n = normed[pl.ds(step * 4, 4)].reshape(4 * COLS, CH)
        gate[pl.ds(step * 4, 4)] = sigmoid(dot(n, gw[u], NN)).reshape(4, COLS, CH)

    def back_group(u, g):
        base = g * GROUP
        back_rows(
            m_in[u, :, pl.ds(pl.multiple_of(base, GROUP), GROUP), :],
            cur.at[u, pl.ds(base, GROUP)],
            gate.at[pl.ds(base, GROUP)],
            cur.at[1 - u, pl.ds(base, GROUP)],
            gain_t.at[u], bias_t.at[u], ow.at[u], tl, ts,
        )

    def loop(count, body):
        def step(i, carry):
            body(i)
            return carry

        lax.fori_loop(0, count, step, 0)

    def rows_of(flight):
        return (*SIDES, *MIXED)[flight][2]

    def spread(flight, g=0):
        if flight < len(SIDES):
            u, first, rows = SIDES[flight]
            part = pl.ds(first + g * rows, rows)
            src_at = lambda r, c: sides.at[u, r * N_COL + c, part]
            dst = all_sides.at[u, col, row, part]
        else:
            u, first, rows = MIXED[flight - len(SIDES)]
            part = pl.ds(first, rows)
            src_at = lambda r, c: m_all.at[u, c, r, part]
            dst = last_mixed.at[me] if flight == FLIGHTS - 1 else m_in.at[u, me, part]
        flight = flight + g
        pltpu.make_async_copy(src_at(row, col), dst, recv_sem.at[flight]).start()

        def send(r, c):
            pltpu.make_async_remote_copy(
                src_ref=src_at(r, c),
                dst_ref=dst,
                send_sem=send_sem.at[flight],
                recv_sem=recv_sem.at[flight],
                device_id=(r, c),
                device_id_type=pl.DeviceIdType.MESH,
            ).start()

        each_target(row, col, send)

    def arrived(flight, g=0):
        size = m_in.at[0, :, pl.ds(0, rows_of(flight))]
        pltpu.make_async_copy(size, size, recv_sem.at[flight + g]).wait()

    def sent(flight):
        size = m_in.at[0, pl.ds(0, DEV - 1), pl.ds(0, rows_of(flight))]
        pltpu.make_async_copy(size, size, send_sem.at[flight]).wait()

    def put_mixed(u, half, jb, out):
        out = out.astype(BF16)
        for k in range(2):
            m_all[u, 2 * jb + k, :, pl.ds(half * HALF, HALF), :] = out[
                :, k * COLS : (k + 1) * COLS
            ].reshape(N_ROW, HALF, COLS)

    def side_rows(u, c, k, half, part, rows=GROUP):
        first = PLACE[u][k, half, part]
        return all_sides[u, c, :, first : first + rows, :].reshape(N_ROW * rows, COLS)

    def mix_outgoing(half):
        a = jnp.concatenate(
            [
                side_rows(0, c, LEFT, half, 0, HALF)
                for c in range(N_COL)
            ],
            axis=1,
        )

        def block(jb):
            b = jnp.concatenate(
                [all_sides[0, c, pl.ds(4 * jb, 4), 0:64].reshape(256, COLS) for c in range(N_COL)],
                axis=1,
            )
            put_mixed(0, half, jb, dot(a, b, NT))

        loop(4, block)

    def turn(half, part):
        def block(c):
            t = side_rows(1, c, LEFT, half, part).T
            for r in range(2):
                lt[half, pl.ds(2 * c, 2), part * HALF : (part + 1) * HALF, r * 256 : r * 256 + 256] = (
                    t[r * 64 : (r + 1) * 64].reshape(2, HALF, 256)
                )

        loop(N_COL, block)

    def mix_incoming(half, k):
        a = lt[k, :, half * HALF : (half + 1) * HALF, :].reshape(512, 512)

        def block(jb):
            b = jnp.concatenate(
                [
                    jnp.concatenate(
                        [
                            side_rows(1, 2 * jb + c, RIGHT, k, r) for r in range(2)
                        ],
                        axis=0,
                    )
                    for c in range(2)
                ],
                axis=1,
            )
            if k == 0:
                acc[half, jb] = dot(a, b, NN)
            else:
                put_mixed(1, half, jb, acc[half, jb] + dot(a, b, NN))

        loop(4, block)

    load(0).wait()
    front_group(0, RIGHT, 0, 0)
    pl.semaphore_wait(barrier, DEV - 1)
    spread(0)
    for copy in params[3:]:
        copy.wait()
    load(1).wait()
    front_group(0, RIGHT, 0, 1)
    spread(1)
    load(2).wait()
    load(3).wait()
    loop(2, lambda g: front_group(0, RIGHT, 1, g))
    spread(2)
    for k in range(2):
        wt[0, k * CH : (k + 1) * CH] = pw[0, k].T
    for half in range(2):
        loop(2, lambda g: front_group(0, LEFT, half, g, False))
        spread(3 + half)
    for k in range(4):
        wt[1, k * CH : (k + 1) * CH] = pw[1, k].T
    for u in range(2):
        gain_t[u] = jnp.broadcast_to(og[u : u + 1], (CH, CH)).T
        bias_t[u] = jnp.broadcast_to(ob[u : u + 1], (CH, CH)).T
    loop(ROWS // 4, lambda s: gate_rows(0, s))
    for flight in range(3):
        arrived(flight)
    for half in range(2):
        arrived(3 + half)
        mix_outgoing(half)
        spread(12 + 2 * half)
        spread(13 + 2 * half)
    for half in range(2):

        def turnover(g):
            arrived(12 + 2 * half, g)
            back_group(0, 2 * half + g)
            front_group(1, RIGHT, half, g)
            if half == 0:
                spread(5, g)

        loop(2, turnover)
        if half == 1:
            spread(8)
        left_by_parts(half)
        spread(7 if half == 0 else 9)
    spread(10)
    spread(11)
    loop(ROWS // 4, lambda s: gate_rows(1, s))
    last = pl.ds(HALF + GROUP, GROUP)
    ahead = [
        pltpu.make_async_copy(src, dst, ahead_sem.at[k])
        for k, (src, dst) in enumerate(((gate.at[last], last_gate), (cur.at[1, last], last_cur)))
    ]
    for copy in ahead:
        copy.start()
    for flight in range(5, 8):
        arrived(flight)
    turn(0, 0)
    mix_incoming(0, 0)
    arrived(8)
    arrived(9)
    turn(1, 0)
    mix_incoming(0, 1)
    spread(16)
    for k in range(2):
        arrived(10 + k)
        turn(k, 1)
        mix_incoming(1, k)
    spread(17)
    spread(18)

    def store(k, first, count):
        rows = pl.ds(first, count)
        return pltpu.make_async_copy(cur.at[0, rows], out_h.at[rows], out_sem.at[k])

    stores = [store(0, 0, HALF), store(1, HALF, GROUP)]
    arrived(16)
    loop(2, lambda g: back_group(1, g))
    stores[0].start()
    arrived(17)
    loop(1, lambda g: back_group(1, 2))
    stores[1].start()
    for flight in range(FLIGHTS):
        sent(flight)
    for copy in ahead + stores:
        copy.wait()
    arrived(18)


def finish(
    done_h, mixed_h, gate_h, cur_h, og_h, ob_h, ow_h, out_h,
    done, mixed, gate, cur, og, ob, ow, new, gain_t, bias_t, tl, ts, sem, out_sem,
):
    loads = [
        pltpu.make_async_copy(src, dst, sem.at[k])
        for k, (src, dst) in enumerate(
            (
                (mixed_h, mixed), (og_h, og), (ob_h, ob), (ow_h, ow), (cur_h, cur), (gate_h, gate),
                *((done_h.at[pl.ds(g * 16, 16)], done.at[pl.ds(g * 16, 16)]) for g in range(3)),
            )
        )
    ]
    for copy in loads[:6]:
        copy.start()
    for copy in loads[1:4]:
        copy.wait()
    gain_t[...] = jnp.broadcast_to(og[1:2], (CH, CH)).T
    bias_t[...] = jnp.broadcast_to(ob[1:2], (CH, CH)).T
    carried = [
        pltpu.make_async_copy(
            done.at[pl.ds(g * 16, 16)], out_h.at[pl.ds(g * 16, 16)], out_sem.at[g]
        )
        for g in range(3)
    ]
    loads[0].wait()
    for copy in loads[6:]:
        copy.start()
    for copy in loads[4:6]:
        copy.wait()
    back_rows(mixed[...], cur, gate, new, gain_t, bias_t, ow.at[1], tl, ts)
    for g in range(3):
        loads[6 + g].wait()
        carried[g].start()
    end = pltpu.make_async_copy(new, out_h.at[pl.ds(48, 16)], out_sem.at[3])
    end.start()
    for copy in (*carried, end):
        copy.wait()


def shards(*args):
    pieces = (2, DEV, ROWS, COLS)
    planes = (2, N_COL, N_ROW, ROWS, COLS)
    vmem = pltpu.VMEM
    scratch = [
        vmem((2, ROWS, COLS, CH), BF16),
        vmem((ROWS, COLS, CH), BF16),
        vmem((ROWS, COLS, CH), F32),
        vmem((2, DEV, 2 * ROWS, COLS), BF16),
        vmem((2, N_COL, N_ROW, 2 * ROWS, COLS), BF16),
        vmem((2, N_ROW, ROWS, 512), BF16),
        vmem((2, 4, 512, 256), F32),
        vmem(planes, BF16),
        vmem(pieces, BF16),
    ]
    scratch += [vmem(a.shape, a.dtype) for a in args[1:]]
    scratch += [
        vmem((2, 4 * CH, CH), BF16),
        vmem((2, CH, CH), F32),
        vmem((2, CH, CH), F32),
        vmem((CH * GROUP, COLS), F32),
        vmem((CH * GROUP, COLS), F32),
        vmem((GROUP, COLS), F32),
        pltpu.SemaphoreType.DMA((ROWS // GROUP,)),
        pltpu.SemaphoreType.DMA((9,)),
        pltpu.SemaphoreType.DMA((FLIGHTS,)),
        pltpu.SemaphoreType.DMA((FLIGHTS,)),
        pltpu.SemaphoreType.DMA((2,)),
        pltpu.SemaphoreType.DMA((2,)),
    ]
    quarter = (GROUP, COLS, CH)
    of_kernel = [
        jax.ShapeDtypeStruct((ROWS - GROUP, COLS, CH), BF16),
        jax.ShapeDtypeStruct((DEV, GROUP, COLS), BF16),
        jax.ShapeDtypeStruct(quarter, F32),
        jax.ShapeDtypeStruct(quarter, BF16),
    ]
    parts = pl.pallas_call(
        kernel,
        out_shape=of_kernel,
        in_specs=[pl.BlockSpec(memory_space=pl.ANY)] * 8,
        out_specs=[pl.BlockSpec(memory_space=pl.ANY)] * 4,
        scratch_shapes=scratch,
        compiler_params=pltpu.CompilerParams(
            collective_id=0, has_side_effects=True, vmem_limit_bytes=60 * MIB
        ),
        name="triangle",
    )(*args)
    ends = args[5:]
    return pl.pallas_call(
        finish,
        out_shape=jax.ShapeDtypeStruct((ROWS, COLS, CH), BF16),
        in_specs=[pl.BlockSpec(memory_space=pl.ANY)] * 7,
        out_specs=pl.BlockSpec(memory_space=pl.ANY),
        scratch_shapes=[vmem(a.shape, a.dtype) for a in (*of_kernel, *ends)]
        + [
            vmem(quarter, BF16),
            vmem((CH, CH), F32),
            vmem((CH, CH), F32),
            vmem((CH * GROUP, COLS), F32),
            vmem((GROUP, COLS), F32),
            pltpu.SemaphoreType.DMA((9,)),
            pltpu.SemaphoreType.DMA((4,)),
        ],
        compiler_params=pltpu.CompilerParams(vmem_limit_bytes=60 * MIB),
        name="finish",
    )(*parts, *ends)


def solution(mesh):
    placed = (P("row", "col", None), P(), P(), P(), P(), P(), P(), P())
    return jax.shard_map(
        shards, mesh=mesh, in_specs=placed, out_specs=P("row", "col", None), check_vma=False
    )
```

profile of v0, /device:TPU:1, one launch (start us, length us, event | category | flops | bytes accessed | tf_op | source)
XLA Modules:
  0.0 153.7 jit_solution(4984386371803213014)
XLA Ops:
  0.0 149.5 %triangle.1 = (bf16[48,128,128]{2,1,0:T(8,128)(2,1)}, bf16[128,16,128]{2,1,0:T(8,128)(2,1)}, f32[16,128,128]{2,1,0:T(8,128)}, bf16[16,128,128]{2,1,0:T(8,128)(2,1)}) custom-call(bf16[64,128,128]{2,1,0:T(8,128)(2,1)} %pair_h.1, f32[2,128]{1,0:T(2,128)} %ng_h.1, f32[2,128]{1,0:T(2,128)} %nb_h.1, bf16[2,4,128,128]{3,2,1,0:T(8,128)(2,1)} %pw_h.1, ...), custom_call_target="tpu_custom_call" | custom-call | tf_op jit(solution)/shard_map/triangle/pallas_call | solution.py:477
  149.5 4.0 %finish.1 = bf16[64,128,128]{2,1,0:T(8,128)(2,1)} custom-call(bf16[48,128,128]{2,1,0:T(8,128)(2,1)} %get-tuple-element.9.done_h, bf16[128,16,128]{2,1,0:T(8,128)(2,1)} %get-tuple-element.10.mixed_h, f32[16,128,128]{2,1,0:T(8,128)} %get-tuple-element.11.gate_h, bf16[16,128,128]{2,1,0:T(8,128)(2,1)} %get-tuple-element.12.cur_h, f32[2,128]{1,0:T(2,128)} %og_h.3, ...), custom_call_target="tpu_custom_call" | custom-call | tf_op jit(solution)/shard_map/finish/pallas_call | solution.py:489
where the time goes:
time: 154 us
  Pallas kernels  154 us (100%)
    pallas_call x1, Pallas kernels, shards(): pl.pallas_call(kernel, out_shape=of_kernel, in_specs=[pl.BlockSpec(memory...  150 us
    pallas_call x1, Pallas kernels, shards(): pl.pallas_call(finish, out_shape=jax.ShapeDtypeStruct((ROWS, COLS, CH), B...  4 us

commit v1 on v0

--- a/solution.py
+++ b/solution.py
@@ -14,25 +14,13 @@
 TN = (((0,), (0,)), ((), ()))
 NN = (((1,), (0,)), ((), ()))
 RIGHT, LEFT = 0, 1
-PLACE = (
-    {(k, half, g): 64 * k + 32 * half + 16 * g for k in range(2) for half in range(2) for g in range(2)},
-    {
-        (RIGHT, 0, 0): 0,
-        (RIGHT, 0, 1): 16,
-        (LEFT, 0, 0): 32,
-        (RIGHT, 1, 0): 48,
-        (RIGHT, 1, 1): 64,
-        (LEFT, 1, 0): 80,
-        (LEFT, 0, 1): 96,
-        (LEFT, 1, 1): 112,
-    },
+SIDES = (
+    (0, 0, 16), (0, 16, 16), (0, 32, 16), (0, 48, 16), (0, 64, 32), (0, 96, 32),
+    (1, 0, 32), (1, 48, 32), (1, 32, 16), (1, 80, 16), (1, 96, 32),
 )
-SIDES = (
-    (0, 0, 16), (0, 16, 16), (0, 32, 32), (0, 64, 32), (0, 96, 32),
-    (1, 0, 16), (1, 16, 16), (1, 32, 16), (1, 48, 32), (1, 80, 16), (1, 96, 16), (1, 112, 16),
-)
-MIXED = ((0, 0, 16), (0, 16, 16), (0, 32, 16), (0, 48, 16), (1, 0, 32), (1, 32, 16), (1, 48, 16))
+MIXED = ((0, 0, 32), (0, 32, 32), (1, 0, 32), (1, 32, 16), (1, 48, 16))
 FLIGHTS = len(SIDES) + len(MIXED)
+FIRST_RIGHT, FIRST_LEFT, NEXT_RIGHT, NEXT_LEFT, LAST_LEFT, FIRST_MIXED, NEXT_MIXED = 0, 4, 6, 8, 10, 11, 13
 
 
 def sigmoid(v):
@@ -77,13 +65,15 @@
     lax.fori_loop(1, 8, step, 0)
 
 
-def back_rows(mixed, cur, gate, new, gain_t, bias_t, weight, tl, ts):
+def back_rows(mixed, cur, gate, new, gain_t, bias_t, weight, tl, ts, ready=None):
     m = mixed.astype(F32)
     mean = jnp.mean(m, axis=0)
     centred = m - mean[None]
     var = jnp.mean(centred * centred, axis=0)
     ts[...] = lax.rsqrt(var + 1e-5)
     tl[...] = centred.reshape(CH * GROUP, COLS)
+    if ready is not None:
+        ready()
     for i in range(GROUP):
         c = tl[pl.ds(i, CH, stride=GROUP), :]
         nm = (c * ts[pl.ds(i, 1), :] * gain_t[...] + bias_t[...]).astype(BF16)
@@ -153,15 +143,11 @@
         p = dot(wt[u, first : first + 256], n, NT)
         return sigmoid(p[0:128]) * p[128:256]
 
-    def keep(u, k, half, g, wide):
-        first = PLACE[u][k, half, 0] + g * GROUP
-        if (u, k) == (1, LEFT):
-            first = PLACE[u][k, half, g]
+    def keep(u, first, wide):
         rows = pl.ds(pl.multiple_of(first, GROUP), GROUP)
         sides[u, :, rows, :] = wide[...].reshape(CH, GROUP, COLS).astype(BF16)
 
-    def front_group(u, k, half, g, fresh=True):
-        base = half * HALF + g * GROUP
+    def front_group(u, k, base, first, fresh=True):
         for i in range(0, GROUP, 2):
             if fresh:
                 n = norm_rows(u, base + i)
@@ -170,7 +156,7 @@
             side = project(u, k, n)
             for r in range(2):
                 (tr, tl)[k][pl.ds(i + r, CH, stride=GROUP), :] = side[:, r * COLS : (r + 1) * COLS]
-        keep(u, k, half, g, (tr, tl)[k])
+        keep(u, first, (tr, tl)[k])
 
     def left_by_parts(half):
         def eight(p):
@@ -185,8 +171,8 @@
                     ]
 
         loop(2, eight)
-        keep(1, LEFT, half, 0, tl)
-        keep(1, LEFT, half, 1, tr)
+        keep(1, half * 48 + 32, tl)
+        keep(1, half * 16 + 96, tr)
 
     def gate_rows(u, step):
         n = normed[pl.ds(step * 4, 4)].reshape(4 * COLS, CH)
@@ -213,25 +199,27 @@
         return (*SIDES, *MIXED)[flight][2]
 
     def spread(flight, g=0):
+        u, first, rows = (*SIDES, *MIXED)[flight]
+        if isinstance(g, int) and g == 0:
+            start = first
+        else:
+            start = pl.multiple_of(first + g * ((*SIDES, *MIXED)[flight + 1][1] - first), GROUP)
+        part = pl.ds(start, rows)
         if flight < len(SIDES):
-            u, first, rows = SIDES[flight]
-            part = pl.ds(first + g * rows, rows)
             src_at = lambda r, c: sides.at[u, r * N_COL + c, part]
             dst = all_sides.at[u, col, row, part]
         else:
-            u, first, rows = MIXED[flight - len(SIDES)]
-            part = pl.ds(first, rows)
             src_at = lambda r, c: m_all.at[u, c, r, part]
             dst = last_mixed.at[me] if flight == FLIGHTS - 1 else m_in.at[u, me, part]
-        flight = flight + g
-        pltpu.make_async_copy(src_at(row, col), dst, recv_sem.at[flight]).start()
+        index = flight + g
+        pltpu.make_async_copy(src_at(row, col), dst, recv_sem.at[index]).start()
 
         def send(r, c):
             pltpu.make_async_remote_copy(
                 src_ref=src_at(r, c),
                 dst_ref=dst,
-                send_sem=send_sem.at[flight],
-                recv_sem=recv_sem.at[flight],
+                send_sem=send_sem.at[index],
+                recv_sem=recv_sem.at[index],
                 device_id=(r, c),
                 device_id_type=pl.DeviceIdType.MESH,
             ).start()
@@ -248,23 +236,18 @@
 
     def put_mixed(u, half, jb, out):
         out = out.astype(BF16)
+        rows = pl.ds(half * HALF, HALF)
         for k in range(2):
-            m_all[u, 2 * jb + k, :, pl.ds(half * HALF, HALF), :] = out[
-                :, k * COLS : (k + 1) * COLS
-            ].reshape(N_ROW, HALF, COLS)
-
-    def side_rows(u, c, k, half, part, rows=GROUP):
-        first = PLACE[u][k, half, part]
-        return all_sides[u, c, :, first : first + rows, :].reshape(N_ROW * rows, COLS)
+            m_all[u, 2 * jb + k, :, rows, :] = out[:, k * COLS : (k + 1) * COLS].reshape(
+                N_ROW, HALF, COLS
+            )
+
+    def side_rows(u, c, first, rows=GROUP):
+        return all_sides[u, c, :, pl.ds(first, rows), :].reshape(N_ROW * rows, COLS)
 
     def mix_outgoing(half):
-        a = jnp.concatenate(
-            [
-                side_rows(0, c, LEFT, half, 0, HALF)
-                for c in range(N_COL)
-            ],
-            axis=1,
-        )
+        first = pl.multiple_of(64 + half * HALF, HALF)
+        a = jnp.concatenate([side_rows(0, c, first, HALF) for c in range(N_COL)], axis=1)
 
         def block(jb):
             b = jnp.concatenate(
@@ -277,7 +260,7 @@
 
     def turn(half, part):
         def block(c):
-            t = side_rows(1, c, LEFT, half, part).T
+            t = side_rows(1, c, half * 48 + 32 if part == 0 else half * 16 + 96).T
             for r in range(2):
                 lt[half, pl.ds(2 * c, 2), part * HALF : (part + 1) * HALF, r * 256 : r * 256 + 256] = (
                     t[r * 64 : (r + 1) * 64].reshape(2, HALF, 256)
@@ -293,7 +276,7 @@
                 [
                     jnp.concatenate(
                         [
-                            side_rows(1, 2 * jb + c, RIGHT, k, r) for r in range(2)
+                            side_rows(1, 2 * jb + c, k * 48 + r * GROUP) for r in range(2)
                         ],
                         axis=0,
                     )
@@ -308,53 +291,62 @@
 
         loop(4, block)
 
-    load(0).wait()
-    front_group(0, RIGHT, 0, 0)
-    pl.semaphore_wait(barrier, DEV - 1)
-    spread(0)
+
+    def open_right(g):
+        load(g).wait()
+        front_group(0, RIGHT, g * GROUP, g * GROUP)
+
+        @pl.when(g == 0)
+        def _():
+            pl.semaphore_wait(barrier, DEV - 1)
+
+        spread(FIRST_RIGHT, g)
+
+    loop(ROWS // GROUP, open_right)
     for copy in params[3:]:
         copy.wait()
-    load(1).wait()
-    front_group(0, RIGHT, 0, 1)
-    spread(1)
-    load(2).wait()
-    load(3).wait()
-    loop(2, lambda g: front_group(0, RIGHT, 1, g))
-    spread(2)
     for k in range(2):
         wt[0, k * CH : (k + 1) * CH] = pw[0, k].T
-    for half in range(2):
-        loop(2, lambda g: front_group(0, LEFT, half, g, False))
-        spread(3 + half)
+
+    def open_left(half):
+        def group(g):
+            base = half * HALF + g * GROUP
+            front_group(0, LEFT, base, 64 + base, False)
+
+        loop(2, group)
+        spread(FIRST_LEFT, half)
+
+    loop(2, open_left)
     for k in range(4):
         wt[1, k * CH : (k + 1) * CH] = pw[1, k].T
     for u in range(2):
         gain_t[u] = jnp.broadcast_to(og[u : u + 1], (CH, CH)).T
         bias_t[u] = jnp.broadcast_to(ob[u : u + 1], (CH, CH)).T
     loop(ROWS // 4, lambda s: gate_rows(0, s))
-    for flight in range(3):
-        arrived(flight)
-    for half in range(2):
-        arrived(3 + half)
+    for g in range(ROWS // GROUP):
+        arrived(FIRST_RIGHT, g)
+
+    def outgoing(half):
+        arrived(FIRST_LEFT, half)
         mix_outgoing(half)
-        spread(12 + 2 * half)
-        spread(13 + 2 * half)
-    for half in range(2):
-
-        def turnover(g):
-            arrived(12 + 2 * half, g)
+        spread(FIRST_MIXED, half)
+
+    loop(2, outgoing)
+
+    def turnover(half):
+        arrived(FIRST_MIXED, half)
+
+        def group(g):
             back_group(0, 2 * half + g)
-            front_group(1, RIGHT, half, g)
-            if half == 0:
-                spread(5, g)
-
-        loop(2, turnover)
-        if half == 1:
-            spread(8)
+            front_group(1, RIGHT, half * HALF + g * GROUP, half * 48 + g * GROUP)
+
+        loop(2, group)
+        spread(NEXT_RIGHT, half)
         left_by_parts(half)
-        spread(7 if half == 0 else 9)
-    spread(10)
-    spread(11)
+        spread(NEXT_LEFT, half)
+
+    loop(2, turnover)
+    spread(LAST_LEFT)
     loop(ROWS // 4, lambda s: gate_rows(1, s))
     last = pl.ds(HALF + GROUP, GROUP)
     ahead = [
@@ -363,38 +355,41 @@
     ]
     for copy in ahead:
         copy.start()
-    for flight in range(5, 8):
-        arrived(flight)
-    turn(0, 0)
-    mix_incoming(0, 0)
-    arrived(8)
-    arrived(9)
-    turn(1, 0)
-    mix_incoming(0, 1)
-    spread(16)
-    for k in range(2):
-        arrived(10 + k)
-        turn(k, 1)
-        mix_incoming(1, k)
-    spread(17)
-    spread(18)
-
-    def store(k, first, count):
-        rows = pl.ds(first, count)
-        return pltpu.make_async_copy(cur.at[0, rows], out_h.at[rows], out_sem.at[k])
-
-    stores = [store(0, 0, HALF), store(1, HALF, GROUP)]
-    arrived(16)
-    loop(2, lambda g: back_group(1, g))
-    stores[0].start()
-    arrived(17)
-    loop(1, lambda g: back_group(1, 2))
-    stores[1].start()
+    for half in range(2):
+        arrived(NEXT_RIGHT, half)
+        arrived(NEXT_LEFT, half)
+        turn(half, 0)
+        mix_incoming(0, half)
+    spread(NEXT_MIXED)
+    arrived(LAST_LEFT)
+    for half in range(2):
+        turn(half, 1)
+        mix_incoming(1, half)
+    spread(NEXT_MIXED + 1)
+    spread(NEXT_MIXED + 2)
+
+    def store(g):
+        rows = pl.ds(g * GROUP, GROUP)
+        return pltpu.make_async_copy(cur.at[0, rows], out_h.at[rows], out_sem.at[g])
+
+    def close(g):
+        @pl.when(g == 0)
+        def _():
+            arrived(NEXT_MIXED)
+
+        @pl.when(g == 2)
+        def _():
+            arrived(NEXT_MIXED + 1)
+
+        back_group(1, g)
+        store(g).start()
+
+    loop(3, close)
     for flight in range(FLIGHTS):
         sent(flight)
-    for copy in ahead + stores:
+    for copy in (*ahead, store(0), store(1), store(2)):
         copy.wait()
-    arrived(18)
+    arrived(NEXT_MIXED + 2)
 
 
 def finish(
@@ -410,7 +405,7 @@
             )
         )
     ]
-    for copy in loads[:6]:
+    for copy in loads:
         copy.start()
     for copy in loads[1:4]:
         copy.wait()
@@ -423,14 +418,15 @@
         for g in range(3)
     ]
     loads[0].wait()
-    for copy in loads[6:]:
-        copy.start()
-    for copy in loads[4:6]:
-        copy.wait()
-    back_rows(mixed[...], cur, gate, new, gain_t, bias_t, ow.at[1], tl, ts)
-    for g in range(3):
-        loads[6 + g].wait()
-        carried[g].start()
+
+    def ready():
+        for copy in loads[4:6]:
+            copy.wait()
+        for g in range(3):
+            loads[6 + g].wait()
+            carried[g].start()
+
+    back_rows(mixed[...], cur, gate, new, gain_t, bias_t, ow.at[1], tl, ts, ready)
     end = pltpu.make_async_copy(new, out_h.at[pl.ds(48, 16)], out_sem.at[3])
     end.start()
     for copy in (*carried, end):
@@ -464,7 +460,7 @@
         pltpu.SemaphoreType.DMA((9,)),
         pltpu.SemaphoreType.DMA((FLIGHTS,)),
         pltpu.SemaphoreType.DMA((FLIGHTS,)),
-        pltpu.SemaphoreType.DMA((2,)),
+        pltpu.SemaphoreType.DMA((3,)),
         pltpu.SemaphoreType.DMA((2,)),
     ]
     quarter = (GROUP, COLS, CH)

time: 154 us -> 153 us (level)
  no operation moved by 1% of the time
where the time goes in v1:
time: 153 us
  Pallas kernels  153 us (100%)
    pallas_call x1, Pallas kernels, shards(): pl.pallas_call(kernel, out_shape=of_kernel, in_specs=[pl.BlockSpec(memory...  149 us
    pallas_call x1, Pallas kernels, shards(): pl.pallas_call(finish, out_shape=jax.ShapeDtypeStruct((ROWS, COLS, CH), B...  3.51 us

profile of v1, /device:TPU:1, one launch (start us, length us, event | category | flops | bytes accessed | tf_op | source)
XLA Modules:
  0.0 153.0 jit_solution(7751576328262802503)
XLA Ops:
  0.0 149.5 %triangle.1 = (bf16[48,128,128]{2,1,0:T(8,128)(2,1)}, bf16[128,16,128]{2,1,0:T(8,128)(2,1)}, f32[16,128,128]{2,1,0:T(8,128)}, bf16[16,128,128]{2,1,0:T(8,128)(2,1)}) custom-call(bf16[64,128,128]{2,1,0:T(8,128)(2,1)} %pair_h.1, f32[2,128]{1,0:T(2,128)} %ng_h.1, f32[2,128]{1,0:T(2,128)} %nb_h.1, bf16[2,4,128,128]{3,2,1,0:T(8,128)(2,1)} %pw_h.1, ...), custom_call_target="tpu_custom_call" | custom-call | tf_op jit(solution)/shard_map/triangle/pallas_call | solution.py:473
  149.5 3.5 %finish.1 = bf16[64,128,128]{2,1,0:T(8,128)(2,1)} custom-call(bf16[48,128,128]{2,1,0:T(8,128)(2,1)} %get-tuple-element.9.done_h, bf16[128,16,128]{2,1,0:T(8,128)(2,1)} %get-tuple-element.10.mixed_h, f32[16,128,128]{2,1,0:T(8,128)} %get-tuple-element.11.gate_h, bf16[16,128,128]{2,1,0:T(8,128)(2,1)} %get-tuple-element.12.cur_h, f32[2,128]{1,0:T(2,128)} %og_h.3, ...), custom_call_target="tpu_custom_call" | custom-call | tf_op jit(solution)/shard_map/finish/pallas_call | solution.py:485

commit v2 on v1

--- a/solution.py
+++ b/solution.py
@@ -65,13 +65,13 @@
     lax.fori_loop(1, 8, step, 0)
 
 
-def back_rows(mixed, cur, gate, new, gain_t, bias_t, weight, tl, ts, ready=None):
+def back_rows(mixed, cur, gate, new, gain_t, bias_t, weight, tl, ts, ready=None, after=None):
     m = mixed.astype(F32)
     mean = jnp.mean(m, axis=0)
     centred = m - mean[None]
     var = jnp.mean(centred * centred, axis=0)
     ts[...] = lax.rsqrt(var + 1e-5)
-    tl[...] = centred.reshape(CH * GROUP, COLS)
+    tl[0 : CH * GROUP] = centred.reshape(CH * GROUP, COLS)
     if ready is not None:
         ready()
     for i in range(GROUP):
@@ -79,6 +79,8 @@
         nm = (c * ts[pl.ds(i, 1), :] * gain_t[...] + bias_t[...]).astype(BF16)
         change = dot(nm, weight[...], TN)
         new[i] = (cur[i].astype(F32) + gate[i] * change).astype(BF16)
+        if after is not None:
+            after(i)
 
 
 def kernel(
@@ -114,19 +116,19 @@
     load(0).start()
     for copy in params[:3]:
         copy.start()
+
+    barrier = pltpu.get_barrier_semaphore()
+
+    def greet(r, c):
+        pl.semaphore_signal(
+            barrier, inc=1, device_id=(r, c), device_id_type=pl.DeviceIdType.MESH
+        )
+
+    each_target(row, col, greet)
     for g in range(1, ROWS // GROUP):
         load(g).start()
     for copy in params[3:]:
         copy.start()
-
-    barrier = pltpu.get_barrier_semaphore()
-
-    def greet(r, c):
-        pl.semaphore_signal(
-            barrier, inc=1, device_id=(r, c), device_id_type=pl.DeviceIdType.MESH
-        )
-
-    each_target(row, col, greet)
     for copy in params[:3]:
         copy.wait()
     for k in range(2, 4):
@@ -145,7 +147,7 @@
 
     def keep(u, first, wide):
         rows = pl.ds(pl.multiple_of(first, GROUP), GROUP)
-        sides[u, :, rows, :] = wide[...].reshape(CH, GROUP, COLS).astype(BF16)
+        sides[u, :, rows, :] = wide[0 : CH * GROUP].reshape(CH, GROUP, COLS).astype(BF16)
 
     def front_group(u, k, base, first, fresh=True):
         for i in range(0, GROUP, 2):
@@ -426,10 +428,19 @@
             loads[6 + g].wait()
             carried[g].start()
 
-    back_rows(mixed[...], cur, gate, new, gain_t, bias_t, ow.at[1], tl, ts, ready)
-    end = pltpu.make_async_copy(new, out_h.at[pl.ds(48, 16)], out_sem.at[3])
-    end.start()
-    for copy in (*carried, end):
+    ends = [
+        pltpu.make_async_copy(
+            new.at[pl.ds(g * 4, 4)], out_h.at[pl.ds(48 + g * 4, 4)], out_sem.at[3 + g]
+        )
+        for g in range(4)
+    ]
+
+    def after(i):
+        if i % 4 == 3:
+            ends[i // 4].start()
+
+    back_rows(mixed[...], cur, gate, new, gain_t, bias_t, ow.at[1], tl, ts, ready, after)
+    for copy in (*carried, *ends):
         copy.wait()
 
 
@@ -453,8 +464,8 @@
         vmem((2, 4 * CH, CH), BF16),
         vmem((2, CH, CH), F32),
         vmem((2, CH, CH), F32),
-        vmem((CH * GROUP, COLS), F32),
-        vmem((CH * GROUP, COLS), F32),
+        vmem((CH * GROUP + GROUP, COLS), F32),
+        vmem((CH * GROUP + GROUP, COLS), F32),
         vmem((GROUP, COLS), F32),
         pltpu.SemaphoreType.DMA((ROWS // GROUP,)),
         pltpu.SemaphoreType.DMA((9,)),
@@ -492,10 +503,10 @@
             vmem(quarter, BF16),
             vmem((CH, CH), F32),
             vmem((CH, CH), F32),
-            vmem((CH * GROUP, COLS), F32),
+            vmem((CH * GROUP + GROUP, COLS), F32),
             vmem((GROUP, COLS), F32),
             pltpu.SemaphoreType.DMA((9,)),
-            pltpu.SemaphoreType.DMA((4,)),
+            pltpu.SemaphoreType.DMA((7,)),
         ],
         compiler_params=pltpu.CompilerParams(vmem_limit_bytes=60 * MIB),
         name="finish",

time: 153 us -> 153 us (level)
  no operation moved by 1% of the time
where the time goes in v2:
time: 153 us
  Pallas kernels  153 us (100%)
    pallas_call x1, Pallas kernels, shards(): pl.pallas_call(kernel, out_shape=of_kernel, in_specs=[pl.BlockSpec(memory...  149 us
    pallas_call x1, Pallas kernels, shards(): pl.pallas_call(finish, out_shape=jax.ShapeDtypeStruct((ROWS, COLS, CH), B...  3.39 us

profile of v2, /device:TPU:1, one launch (start us, length us, event | category | flops | bytes accessed | tf_op | source)
XLA Modules:
  0.0 152.8 jit_solution(4186580676706913006)
XLA Ops:
  0.0 149.4 %triangle.1 = (bf16[48,128,128]{2,1,0:T(8,128)(2,1)}, bf16[128,16,128]{2,1,0:T(8,128)(2,1)}, f32[16,128,128]{2,1,0:T(8,128)}, bf16[16,128,128]{2,1,0:T(8,128)(2,1)}) custom-call(bf16[64,128,128]{2,1,0:T(8,128)(2,1)} %pair_h.1, f32[2,128]{1,0:T(2,128)} %ng_h.1, f32[2,128]{1,0:T(2,128)} %nb_h.1, bf16[2,4,128,128]{3,2,1,0:T(8,128)(2,1)} %pw_h.1, ...), custom_call_target="tpu_custom_call" | custom-call | tf_op jit(solution)/shard_map/triangle/pallas_call | solution.py:484
  149.4 3.4 %finish.1 = bf16[64,128,128]{2,1,0:T(8,128)(2,1)} custom-call(bf16[48,128,128]{2,1,0:T(8,128)(2,1)} %get-tuple-element.9.done_h, bf16[128,16,128]{2,1,0:T(8,128)(2,1)} %get-tuple-element.10.mixed_h, f32[16,128,128]{2,1,0:T(8,128)} %get-tuple-element.11.gate_h, bf16[16,128,128]{2,1,0:T(8,128)(2,1)} %get-tuple-element.12.cur_h, f32[2,128]{1,0:T(2,128)} %og_h.3, ...), custom_call_target="tpu_custom_call" | custom-call | tf_op jit(solution)/shard_map/finish/pallas_call | solution.py:496

commit v3 on v2

--- a/solution.py
+++ b/solution.py
@@ -113,7 +113,9 @@
             )
         )
     ]
-    load(0).start()
+    for k in range(4):
+        rows = pl.ds(4 * k, 4)
+        pltpu.make_async_copy(pair_h.at[rows], cur.at[0, rows], load_sem.at[0]).start()
     for copy in params[:3]:
         copy.start()
 
@@ -398,35 +400,41 @@
     done_h, mixed_h, gate_h, cur_h, og_h, ob_h, ow_h, out_h,
     done, mixed, gate, cur, og, ob, ow, new, gain_t, bias_t, tl, ts, sem, out_sem,
 ):
-    loads = [
-        pltpu.make_async_copy(src, dst, sem.at[k])
-        for k, (src, dst) in enumerate(
-            (
-                (mixed_h, mixed), (og_h, og), (ob_h, ob), (ow_h, ow), (cur_h, cur), (gate_h, gate),
-                *((done_h.at[pl.ds(g * 16, 16)], done.at[pl.ds(g * 16, 16)]) for g in range(3)),
-            )
-        )
-    ]
-    for copy in loads:
+    def in_fours(src, dst, k):
+        count = src.shape[0] // 4
+        for part in range(4):
+            rows = pl.ds(part * count, count)
+            pltpu.make_async_copy(src.at[rows], dst.at[rows], sem.at[k]).start()
+        return pltpu.make_async_copy(src, dst, sem.at[k])
+
+    own_mixed = in_fours(mixed_h, mixed, 0)
+    small = [
+        pltpu.make_async_copy(src, dst, sem.at[1 + k])
+        for k, (src, dst) in enumerate(((og_h, og), (ob_h, ob), (ow_h, ow)))
+    ]
+    for copy in small:
         copy.start()
-    for copy in loads[1:4]:
+    own_cur, own_gate = in_fours(cur_h, cur, 4), in_fours(gate_h, gate, 5)
+    for copy in small:
         copy.wait()
     gain_t[...] = jnp.broadcast_to(og[1:2], (CH, CH)).T
     bias_t[...] = jnp.broadcast_to(ob[1:2], (CH, CH)).T
+    blocks = [pl.ds(g * 16, 16) for g in range(3)]
+    brought = [
+        pltpu.make_async_copy(done_h.at[rows], done.at[rows], sem.at[6 + g])
+        for g, rows in enumerate(blocks)
+    ]
     carried = [
-        pltpu.make_async_copy(
-            done.at[pl.ds(g * 16, 16)], out_h.at[pl.ds(g * 16, 16)], out_sem.at[g]
-        )
-        for g in range(3)
-    ]
-    loads[0].wait()
+        pltpu.make_async_copy(done.at[rows], out_h.at[rows], out_sem.at[g])
+        for g, rows in enumerate(blocks)
+    ]
+    own_mixed.wait()
+    for copy in brought:
+        copy.start()
 
     def ready():
-        for copy in loads[4:6]:
-            copy.wait()
-        for g in range(3):
-            loads[6 + g].wait()
-            carried[g].start()
+        own_cur.wait()
+        own_gate.wait()
 
     ends = [
         pltpu.make_async_copy(
@@ -438,6 +446,9 @@
     def after(i):
         if i % 4 == 3:
             ends[i // 4].start()
+            if i < 12:
+                brought[i // 4].wait()
+                carried[i // 4].start()
 
     back_rows(mixed[...], cur, gate, new, gain_t, bias_t, ow.at[1], tl, ts, ready, after)
     for copy in (*carried, *ends):

time: 153 us -> 153 us (level)
  no operation moved by 1% of the time
where the time goes in v3:
time: 153 us
  Pallas kernels  153 us (100%)
    pallas_call x1, Pallas kernels, shards(): pl.pallas_call(kernel, out_shape=of_kernel, in_specs=[pl.BlockSpec(memory...  149 us
    pallas_call x1, Pallas kernels, shards(): pl.pallas_call(finish, out_shape=jax.ShapeDtypeStruct((ROWS, COLS, CH), B...  3.92 us

profile of v3, /device:TPU:1, one launch (start us, length us, event | category | flops | bytes accessed | tf_op | source)
XLA Modules:
  0.0 153.3 jit_solution(17553419039645209756)
XLA Ops:
  0.0 149.4 %triangle.1 = (bf16[48,128,128]{2,1,0:T(8,128)(2,1)}, bf16[128,16,128]{2,1,0:T(8,128)(2,1)}, f32[16,128,128]{2,1,0:T(8,128)}, bf16[16,128,128]{2,1,0:T(8,128)(2,1)}) custom-call(bf16[64,128,128]{2,1,0:T(8,128)(2,1)} %pair_h.1, f32[2,128]{1,0:T(2,128)} %ng_h.1, f32[2,128]{1,0:T(2,128)} %nb_h.1, bf16[2,4,128,128]{3,2,1,0:T(8,128)(2,1)} %pw_h.1, ...), custom_call_target="tpu_custom_call" | custom-call | tf_op jit(solution)/shard_map/triangle/pallas_call | solution.py:495
  149.4 3.9 %finish.1 = bf16[64,128,128]{2,1,0:T(8,128)(2,1)} custom-call(bf16[48,128,128]{2,1,0:T(8,128)(2,1)} %get-tuple-element.9.done_h, bf16[128,16,128]{2,1,0:T(8,128)(2,1)} %get-tuple-element.10.mixed_h, f32[16,128,128]{2,1,0:T(8,128)} %get-tuple-element.11.gate_h, bf16[16,128,128]{2,1,0:T(8,128)(2,1)} %get-tuple-element.12.cur_h, f32[2,128]{1,0:T(2,128)} %og_h.3, ...), custom_call_target="tpu_custom_call" | custom-call | tf_op jit(solution)/shard_map/finish/pallas_call | solution.py:507

commit v4 on v3

--- a/solution.py
+++ b/solution.py
@@ -428,13 +428,16 @@
         pltpu.make_async_copy(done.at[rows], out_h.at[rows], out_sem.at[g])
         for g, rows in enumerate(blocks)
     ]
-    own_mixed.wait()
     for copy in brought:
         copy.start()
+    own_mixed.wait()
 
     def ready():
         own_cur.wait()
         own_gate.wait()
+        for come, go in zip(brought, carried):
+            come.wait()
+            go.start()
 
     ends = [
         pltpu.make_async_copy(
@@ -446,9 +449,6 @@
     def after(i):
         if i % 4 == 3:
             ends[i // 4].start()
-            if i < 12:
-                brought[i // 4].wait()
-                carried[i // 4].start()
 
     back_rows(mixed[...], cur, gate, new, gain_t, bias_t, ow.at[1], tl, ts, ready, after)
     for copy in (*carried, *ends):

time: 153 us -> 153 us (level)
  no operation moved by 1% of the time
where the time goes in v4:
time: 153 us
  Pallas kernels  153 us (100%)
    pallas_call x1, Pallas kernels, shards(): pl.pallas_call(kernel, out_shape=of_kernel, in_specs=[pl.BlockSpec(memory...  149 us
    pallas_call x1, Pallas kernels, shards(): pl.pallas_call(finish, out_shape=jax.ShapeDtypeStruct((ROWS, COLS, CH), B...  3.95 us

profile of v4, /device:TPU:1, one launch (start us, length us, event | category | flops | bytes accessed | tf_op | source)
XLA Modules:
  0.0 153.3 jit_solution(16299574311740128420)
XLA Ops:
  0.0 149.4 %triangle.1 = (bf16[48,128,128]{2,1,0:T(8,128)(2,1)}, bf16[128,16,128]{2,1,0:T(8,128)(2,1)}, f32[16,128,128]{2,1,0:T(8,128)}, bf16[16,128,128]{2,1,0:T(8,128)(2,1)}) custom-call(bf16[64,128,128]{2,1,0:T(8,128)(2,1)} %pair_h.1, f32[2,128]{1,0:T(2,128)} %ng_h.1, f32[2,128]{1,0:T(2,128)} %nb_h.1, bf16[2,4,128,128]{3,2,1,0:T(8,128)(2,1)} %pw_h.1, ...), custom_call_target="tpu_custom_call" | custom-call | tf_op jit(solution)/shard_map/triangle/pallas_call | solution.py:495
  149.4 4.0 %finish.1 = bf16[64,128,128]{2,1,0:T(8,128)(2,1)} custom-call(bf16[48,128,128]{2,1,0:T(8,128)(2,1)} %get-tuple-element.9.done_h, bf16[128,16,128]{2,1,0:T(8,128)(2,1)} %get-tuple-element.10.mixed_h, f32[16,128,128]{2,1,0:T(8,128)} %get-tuple-element.11.gate_h, bf16[16,128,128]{2,1,0:T(8,128)(2,1)} %get-tuple-element.12.cur_h, f32[2,128]{1,0:T(2,128)} %og_h.3, ...), custom_call_target="tpu_custom_call" | custom-call | tf_op jit(solution)/shard_map/finish/pallas_call | solution.py:507

commit v5 on v2

--- a/solution.py
+++ b/solution.py
@@ -403,7 +403,7 @@
         for k, (src, dst) in enumerate(
             (
                 (mixed_h, mixed), (og_h, og), (ob_h, ob), (ow_h, ow), (cur_h, cur), (gate_h, gate),
-                *((done_h.at[pl.ds(g * 16, 16)], done.at[pl.ds(g * 16, 16)]) for g in range(3)),
+                (done_h, done),
             )
         )
     ]
@@ -413,34 +413,28 @@
         copy.wait()
     gain_t[...] = jnp.broadcast_to(og[1:2], (CH, CH)).T
     bias_t[...] = jnp.broadcast_to(ob[1:2], (CH, CH)).T
-    carried = [
-        pltpu.make_async_copy(
-            done.at[pl.ds(g * 16, 16)], out_h.at[pl.ds(g * 16, 16)], out_sem.at[g]
-        )
-        for g in range(3)
-    ]
+    kept = pl.ds(0, ROWS - GROUP)
+    carried = pltpu.make_async_copy(done, out_h.at[kept], out_sem.at[0])
     loads[0].wait()
 
     def ready():
-        for copy in loads[4:6]:
+        for copy in loads[4:]:
             copy.wait()
-        for g in range(3):
-            loads[6 + g].wait()
-            carried[g].start()
+        carried.start()
 
     ends = [
         pltpu.make_async_copy(
-            new.at[pl.ds(g * 4, 4)], out_h.at[pl.ds(48 + g * 4, 4)], out_sem.at[3 + g]
+            new.at[pl.ds(g * 8, 8)], out_h.at[pl.ds(48 + g * 8, 8)], out_sem.at[1 + g]
         )
-        for g in range(4)
+        for g in range(2)
     ]
 
     def after(i):
-        if i % 4 == 3:
-            ends[i // 4].start()
+        if i % 8 == 7:
+            ends[i // 8].start()
 
     back_rows(mixed[...], cur, gate, new, gain_t, bias_t, ow.at[1], tl, ts, ready, after)
-    for copy in (*carried, *ends):
+    for copy in (carried, *ends):
         copy.wait()
 
 
@@ -505,8 +499,8 @@
             vmem((CH, CH), F32),
             vmem((CH * GROUP + GROUP, COLS), F32),
             vmem((GROUP, COLS), F32),
-            pltpu.SemaphoreType.DMA((9,)),
             pltpu.SemaphoreType.DMA((7,)),
+            pltpu.SemaphoreType.DMA((3,)),
         ],
         compiler_params=pltpu.CompilerParams(vmem_limit_bytes=60 * MIB),
         name="finish",

time: 153 us -> 153 us (level)
  no operation moved by 1% of the time
where the time goes in v5:
time: 153 us
  Pallas kernels  153 us (100%)
    pallas_call x1, Pallas kernels, shards(): pl.pallas_call(kernel, out_shape=of_kernel, in_specs=[pl.BlockSpec(memory...  149 us
    pallas_call x1, Pallas kernels, shards(): pl.pallas_call(finish, out_shape=jax.ShapeDtypeStruct((ROWS, COLS, CH), B...  3.5 us

profile of v5, /device:TPU:1, one launch (start us, length us, event | category | flops | bytes accessed | tf_op | source)
XLA Modules:
  0.0 152.9 jit_solution(12505512467733639926)
XLA Ops:
  0.0 149.4 %triangle.1 = (bf16[48,128,128]{2,1,0:T(8,128)(2,1)}, bf16[128,16,128]{2,1,0:T(8,128)(2,1)}, f32[16,128,128]{2,1,0:T(8,128)}, bf16[16,128,128]{2,1,0:T(8,128)(2,1)}) custom-call(bf16[64,128,128]{2,1,0:T(8,128)(2,1)} %pair_h.1, f32[2,128]{1,0:T(2,128)} %ng_h.1, f32[2,128]{1,0:T(2,128)} %nb_h.1, bf16[2,4,128,128]{3,2,1,0:T(8,128)(2,1)} %pw_h.1, ...), custom_call_target="tpu_custom_call" | custom-call | tf_op jit(solution)/shard_map/triangle/pallas_call | solution.py:478
  149.4 3.5 %finish.1 = bf16[64,128,128]{2,1,0:T(8,128)(2,1)} custom-call(bf16[48,128,128]{2,1,0:T(8,128)(2,1)} %get-tuple-element.9.done_h, bf16[128,16,128]{2,1,0:T(8,128)(2,1)} %get-tuple-element.10.mixed_h, f32[16,128,128]{2,1,0:T(8,128)} %get-tuple-element.11.gate_h, bf16[16,128,128]{2,1,0:T(8,128)(2,1)} %get-tuple-element.12.cur_h, f32[2,128]{1,0:T(2,128)} %og_h.3, ...), custom_call_target="tpu_custom_call" | custom-call | tf_op jit(solution)/shard_map/finish/pallas_call | solution.py:490

commit v6 on v2

--- a/solution.py
+++ b/solution.py
@@ -45,6 +45,8 @@
     turns = [sign * a + 4 for a in range(4)]
     xs = [lax.rem(x + turn, 4) * 2 for turn in turns]
     ys = [lax.rem(y + turn, 4) * 4 for turn in turns]
+    x_of = {(a, d): xs[a] + k * (xs[d] - xs[a]) for a in range(4) for d in range(4)}
+    y_of = {(a, d): ys[d] + k * (ys[a] - ys[d]) for a in range(4) for d in range(4)}
 
     def sixteen(core, c, skip):
         core_at = lax.rem(k + core, 2)
@@ -55,7 +57,7 @@
             for a in range(4):
                 if not (skip and a == 0 and b == 0):
                     ab = (a + b) % 4
-                    body(ys[ab] + z_rows[ab], xs[a] + z_cols[ab])
+                    body(y_of[a, ab] + z_rows[ab], x_of[a, ab] + z_cols[ab])
 
     def step(p, carry):
         sixteen(p // 4, lax.rem(p, 4), False)

time: 153 us -> 153 us (level)
  no operation moved by 1% of the time
where the time goes in v6:
time: 153 us
  Pallas kernels  153 us (100%)
    pallas_call x1, Pallas kernels, shards(): pl.pallas_call(kernel, out_shape=of_kernel, in_specs=[pl.BlockSpec(memory...  150 us
    pallas_call x1, Pallas kernels, shards(): pl.pallas_call(finish, out_shape=jax.ShapeDtypeStruct((ROWS, COLS, CH), B...  3.4 us

profile of v6, /device:TPU:1, one launch (start us, length us, event | category | flops | bytes accessed | tf_op | source)
XLA Modules:
  0.0 153.1 jit_solution(5707628582269617820)
XLA Ops:
  0.0 149.7 %triangle.1 = (bf16[48,128,128]{2,1,0:T(8,128)(2,1)}, bf16[128,16,128]{2,1,0:T(8,128)(2,1)}, f32[16,128,128]{2,1,0:T(8,128)}, bf16[16,128,128]{2,1,0:T(8,128)(2,1)}) custom-call(bf16[64,128,128]{2,1,0:T(8,128)(2,1)} %pair_h.1, f32[2,128]{1,0:T(2,128)} %ng_h.1, f32[2,128]{1,0:T(2,128)} %nb_h.1, bf16[2,4,128,128]{3,2,1,0:T(8,128)(2,1)} %pw_h.1, ...), custom_call_target="tpu_custom_call" | custom-call | tf_op jit(solution)/shard_map/triangle/pallas_call | solution.py:486
  149.7 3.4 %finish.1 = bf16[64,128,128]{2,1,0:T(8,128)(2,1)} custom-call(bf16[48,128,128]{2,1,0:T(8,128)(2,1)} %get-tuple-element.9.done_h, bf16[128,16,128]{2,1,0:T(8,128)(2,1)} %get-tuple-element.10.mixed_h, f32[16,128,128]{2,1,0:T(8,128)} %get-tuple-element.11.gate_h, bf16[16,128,128]{2,1,0:T(8,128)(2,1)} %get-tuple-element.12.cur_h, f32[2,128]{1,0:T(2,128)} %og_h.3, ...), custom_call_target="tpu_custom_call" | custom-call | tf_op jit(solution)/shard_map/finish/pallas_call | solution.py:498

commit v7 on v5

--- a/solution.py
+++ b/solution.py
@@ -418,9 +418,8 @@
     loads[0].wait()
 
     def ready():
-        for copy in loads[4:]:
+        for copy in loads[4:6]:
             copy.wait()
-        carried.start()
 
     ends = [
         pltpu.make_async_copy(
@@ -434,6 +433,8 @@
             ends[i // 8].start()
 
     back_rows(mixed[...], cur, gate, new, gain_t, bias_t, ow.at[1], tl, ts, ready, after)
+    loads[6].wait()
+    carried.start()
     for copy in (carried, *ends):
         copy.wait()
 

time: 153 us -> 153 us (level)
  no operation moved by 1% of the time
where the time goes in v7:
time: 153 us
  Pallas kernels  153 us (100%)
    pallas_call x1, Pallas kernels, shards(): pl.pallas_call(kernel, out_shape=of_kernel, in_specs=[pl.BlockSpec(memory...  149 us
    pallas_call x1, Pallas kernels, shards(): pl.pallas_call(finish, out_shape=jax.ShapeDtypeStruct((ROWS, COLS, CH), B...  3.48 us

profile of v7, /device:TPU:1, one launch (start us, length us, event | category | flops | bytes accessed | tf_op | source)
XLA Modules:
  0.0 152.8 jit_solution(16896238104371707163)
XLA Ops:
  0.0 149.4 %triangle.1 = (bf16[48,128,128]{2,1,0:T(8,128)(2,1)}, bf16[128,16,128]{2,1,0:T(8,128)(2,1)}, f32[16,128,128]{2,1,0:T(8,128)}, bf16[16,128,128]{2,1,0:T(8,128)(2,1)}) custom-call(bf16[64,128,128]{2,1,0:T(8,128)(2,1)} %pair_h.1, f32[2,128]{1,0:T(2,128)} %ng_h.1, f32[2,128]{1,0:T(2,128)} %nb_h.1, bf16[2,4,128,128]{3,2,1,0:T(8,128)(2,1)} %pw_h.1, ...), custom_call_target="tpu_custom_call" | custom-call | tf_op jit(solution)/shard_map/triangle/pallas_call | solution.py:479
  149.4 3.5 %finish.1 = bf16[64,128,128]{2,1,0:T(8,128)(2,1)} custom-call(bf16[48,128,128]{2,1,0:T(8,128)(2,1)} %get-tuple-element.9.done_h, bf16[128,16,128]{2,1,0:T(8,128)(2,1)} %get-tuple-element.10.mixed_h, f32[16,128,128]{2,1,0:T(8,128)} %get-tuple-element.11.gate_h, bf16[16,128,128]{2,1,0:T(8,128)(2,1)} %get-tuple-element.12.cur_h, f32[2,128]{1,0:T(2,128)} %og_h.3, ...), custom_call_target="tpu_custom_call" | custom-call | tf_op jit(solution)/shard_map/finish/pallas_call | solution.py:491
